TPU v7x, 32 devices: a whole 2x2x4 slice. The times are simulated.
32 devices in a mesh: gx: 8 (over z, x), gy: 4 (over y, core).
Axes of the slice: x: 2, y: 2, z: 4, core: 2. Of those that a mesh axis runs over, the one named last changes fastest.
Arguments:
- rhs_field: float32 [2, 8, 64, 1024], P(None, None, 'gx', 'gy'), may hold values from -6 to 6
- permittivity: float32 [8, 64, 1024], P(None, 'gx', 'gy'), may hold values from 1 to 4
- surf_dist: float32 [1024, 128], P(('gx', 'gy')), may hold values from 0.2 to 1
- surf_normal: float32 [3, 1024, 128], P(None, ('gx', 'gy')), may hold values from -4 to 4
- surf_inc: float32 [2, 1024, 128], P(None, ('gx', 'gy')), may hold values from -6 to 6
- surf_cell: int32 [1024, 128], P(('gx', 'gy')), may hold values from 0 to 16383
- surf_mask: int32 [1024, 128], P(('gx', 'gy')), may hold values 0 or 1
- surf_owner: int32 [1024, 1], P(('gx', 'gy')), may hold values from 0 to 31; in each aligned block of 32 rows (0 to 31, 32 to 63, ...) at most 2 rows name the same one
Outputs:
- solution: float32 [2, 8, 64, 1024], P(None, None, 'gx', 'gy')
- residual: float32 [2, 8, 64, 1024], P(None, None, 'gx', 'gy')
Inputs may be any that keep to these rules, and one draw needn't show every extreme that they name: `surf_owner`: within the 32 rows of one device no owner is named more than 2 times, a bound that some block reaches.
All inputs are finite; a program needn't handle non-finite values. No bound on the sum of `surf_mask` on one device may be relied on, other than what follows from the above.
Results may differ from a plain program's by a relative error of at most 0.00002.
Values sent between devices are 32-bit elements; how exact they have to be, the bound alone decides.
A program may use at most 128 MiB of HBM per device.

v0:
```python
import jax
import jax.numpy as jnp
from jax import lax
from jax.sharding import PartitionSpec as P

CAP = 2
ITERS = 2


K_SQUARED = 0.25
BETA = 0.5
OMEGA = 0.8
TAU = 1.0


def with_halo(shard, sides, width):
    for axis, dim in sides:
        size, length = (lax.axis_size(axis), shard.shape[dim])
        up = [(i, (i + 1) % size) for i in range(size - 1)]
        down = [(j, i) for i, j in up]
        last = lax.slice_in_dim(shard, length - width, length, axis=dim)
        first = lax.slice_in_dim(shard, 0, width, axis=dim)
        before = lax.ppermute(last, axis, up)
        after = lax.ppermute(first, axis, down)
        shard = jnp.concatenate([before, shard, after], axis=dim)
    return shard


def padded_field(field):
    framed = with_halo(field, (("gx", 2), ("gy", 3)), 1)
    return jnp.pad(framed, ((0, 0), (1, 1), (0, 0), (0, 0)))


def apply_helm(padded, perm):
    center = padded[:, 1:-1, 1:-1, 1:-1]
    beside = padded[:, 2:, 1:-1, 1:-1] + padded[:, :-2, 1:-1, 1:-1]
    beside = beside + padded[:, 1:-1, 2:, 1:-1] + padded[:, 1:-1, :-2, 1:-1]
    beside = beside + padded[:, 1:-1, 1:-1, 2:] + padded[:, 1:-1, 1:-1, :-2]
    return (6.0 - K_SQUARED * perm)[None] * center - beside


def complex_divide(vec, inv_real, inv_imag):
    return jnp.stack([vec[0] * inv_real - vec[1] * inv_imag, vec[0] * inv_imag + vec[1] * inv_real])


def per_device(
    rhs_field, permittivity, surf_dist, surf_normal, surf_inc, surf_cell, surf_mask, surf_owner
):
    rows_dev = rhs_field.shape[2]
    cols_dev = rhs_field.shape[3]
    planes = rhs_field.shape[1]
    grid_x = lax.axis_size("gx")
    grid_y = lax.axis_size("gy")
    devices = grid_x * grid_y
    points = surf_cell.shape[1]
    owner_ids = surf_owner[:, 0]
    onehot = (owner_ids[:, None] == jnp.arange(devices, dtype=jnp.int32)[None, :]).astype(jnp.int32)
    slot_rank = jnp.sum((jnp.cumsum(onehot, axis=0) - onehot) * onehot, axis=1)
    slot_index = owner_ids * CAP + slot_rank
    float_data = jnp.concatenate([surf_dist[None], surf_normal, surf_inc], axis=0)
    int_data = jnp.stack([surf_cell, surf_mask])
    float_send = (
        jnp.zeros((6, devices * CAP, points), jnp.float32).at[:, slot_index, :].set(float_data)
    )
    int_send = jnp.zeros((2, devices * CAP, points), jnp.int32).at[:, slot_index, :].set(int_data)
    float_recv, int_recv = (
        lax.all_to_all(float_send, ("gx", "gy"), split_axis=1, concat_axis=1, tiled=True),
        lax.all_to_all(int_send, ("gx", "gy"), split_axis=1, concat_axis=1, tiled=True),
    )
    dist = float_recv[0].reshape(-1)
    normal = float_recv[1:4].reshape(3, -1)
    incident = float_recv[4:6].reshape(2, -1)
    cells = int_recv[0].reshape(-1)
    weight = TAU * int_recv[1].reshape(-1).astype(jnp.float32)
    per_plane = rows_dev * cols_dev
    diag_real = 6.0 - K_SQUARED * permittivity
    diag_imag = BETA * K_SQUARED * permittivity
    denom = diag_real * diag_real + diag_imag * diag_imag
    inv_real = diag_real / denom
    inv_imag = -diag_imag / denom
    solution = jnp.zeros_like(rhs_field)
    residual = rhs_field
    for outer_no in range(ITERS):
        padded = padded_field(solution)
        image = apply_helm(padded, permittivity)
        center = padded[:, 1:-1, 1:-1, 1:-1]
        diff_z = padded[:, 2:, 1:-1, 1:-1] - padded[:, :-2, 1:-1, 1:-1]
        diff_x = padded[:, 1:-1, 2:, 1:-1] - padded[:, 1:-1, :-2, 1:-1]
        diff_y = padded[:, 1:-1, 1:-1, 2:] - padded[:, 1:-1, 1:-1, :-2]
        features = jnp.stack([center, diff_z, diff_x, diff_y]).reshape(8, -1)
        picked = jnp.take(features, cells, axis=1).reshape(4, 2, -1)
        grad_dot = normal[0] * picked[1]
        grad_dot = grad_dot + normal[1] * picked[2]
        grad_dot = grad_dot + normal[2] * picked[3]
        penalty = weight * (picked[0] + dist * grad_dot * 0.5 + incident)
        surface = jnp.zeros((2, planes * per_plane), jnp.float32).at[:, cells].add(penalty)
        residual = rhs_field - image - surface.reshape(rhs_field.shape)
        update = OMEGA * complex_divide(residual, inv_real, inv_imag)
        image_z = apply_helm(padded_field(update), permittivity)
        shifted = jnp.stack(
            [image_z[0] - diag_imag * update[1], image_z[1] + diag_imag * update[0]]
        )
        update = update + OMEGA * complex_divide(residual - shifted, inv_real, inv_imag)
        solution = solution + update
    return (solution, residual)


def solution(mesh):
    placed = (
        P(None, None, "gx", "gy"),
        P(None, "gx", "gy"),
        P(("gx", "gy"), None),
        P(None, ("gx", "gy"), None),
        P(None, ("gx", "gy"), None),
        P(("gx", "gy"), None),
        P(("gx", "gy"), None),
        P(("gx", "gy"), None),
    )
    return jax.shard_map(
        per_device,
        mesh=mesh,
        in_specs=placed,
        out_specs=(P(None, None, "gx", "gy"), P(None, None, "gx", "gy")),
        check_vma=False,
    )
```

profile of v0, /device:TPU:3, one launch (start us, length us, event | category | flops | bytes accessed | tf_op | source)
XLA Modules:
  0.0 300.1 jit_solution(10837706097898238646)
XLA Ops:
  0.6 1.9 collective-permute-start.1
  2.6 4.3 %collective-permute-start = (f32[2,8,1,256]{3,2,1,0:T(1,128)S(1)}, f32[2,8,1,256]{3,2,1,0:T(1,128)S(1)}, u32[]{:S(2)}, u32[]{:S(2)}) collective-permute-start(f32[2,8,1,256]{3,2,1,0:T(1,128)S(1)} %broadcast.87), channel_id=1, source_target_pairs={{0,4},{4,8},{8,12},{12,16},{16,20},{20,24},{24,28},{1,5},{5,9},{9,... | collective-permute-start | bytes 49160 | tf_op jit(solution)/shard_map/ppermute | solution.py:23
  6.8 0.7 fusion.47
  7.6 0.8 select_reduce_fusion
  8.5 0.7 fusion.48
  9.1 0.7 add_bitcast_fusion.2
  9.9 0.6 broadcast_in_dim.36
  10.5 3.7 %scatter_fusion = s32[2,64,128]{2,0,1:T(2,128)} fusion(s32[2,64,128]{2,0,1:T(2,128)} %broadcast_in_dim.36, s32[32]{0:T(128)S(1)} %fusion.48, s32[32,2,128]{2,1,0:T(2,128)S(1)} %copy.24), kind=kCustom, calls=%fused_computation.2 | custom fusion | bytes 98432 | tf_op jit(solution)/shard_map/scatter | solution.py:65
  14.2 6.0 %all-to-all-start = ((s32[2,64,128]{2,0,1:T(2,128)}), s32[2,64,128]{2,0,1:T(2,128)S(1)}, u32[]{:S(2)}, u32[]{:S(2)}) async-start(s32[2,64,128]{2,0,1:T(2,128)} %scatter_fusion), calls=%async_computation | async-start | bytes 131072 | tf_op jit(solution)/shard_map/all_to_all | solution.py:68
  20.2 0.9 broadcast_multiply_fusion
  21.3 3.3 %collective-permute-start.2 = (f32[2,8,10,1]{3,2,1,0:T(8,128)S(1)}, f32[2,8,10,1]{3,2,1,0:T(8,128)S(1)}, u32[]{:S(2)}, u32[]{:S(2)}) collective-permute-start(f32[2,8,10,1]{3,2,1,0:T(8,128)S(1)} %get-tuple-element.17), channel_id=1, source_target_pairs={{0,1},{1,2},{2,3},{4,5},{5,6},{6,7},{8,9},{9,10},{10,11},{12,13},{... | collective-permute-start | bytes 1928 | tf_op jit(solution)/shard_map/ppermute | solution.py:23
  24.6 1.9 collective-permute-start.3
  26.6 0.8 maximum_bitcast_fusion
  27.5 0.7 broadcast_in_dim.37
  28.2 3.5 %scatter_fusion.1 = f32[6,64,128]{2,0,1:T(8,128)} fusion(f32[6,64,128]{2,0,1:T(8,128)} %broadcast_in_dim.37, s32[32]{0:T(128)S(1)} %fusion.48, f32[32,6,128]{2,1,0:T(8,128)S(1)} %copy.27), kind=kCustom, calls=%fused_computation.3 | custom fusion | bytes 295040 | tf_op jit(solution)/shard_map/scatter | solution.py:63
  31.7 0.3 select_maximum_fusion.12
  32.0 0.1 subtract_bitcast_fusion.5
  32.2 0.2 subtract_bitcast_fusion.4
  32.4 0.1 pad_maximum_fusion
  32.5 0.1 reshape.132
  32.6 5.3 %copy.25 = f32[8,16384]{0,1:T(8,128)} copy(f32[8,16384]{1,0:T(8,128)S(1)} %reshape.132) | data formatting | bytes 1048576 | tf_op jit(solution)/shard_map/reshape | solution.py:90
  37.9 6.1 %all-to-all-start.1 = ((f32[6,64,128]{2,0,1:T(8,128)}), f32[6,64,128]{2,0,1:T(8,128)S(1)}, u32[]{:S(2)}, u32[]{:S(2)}) async-start(f32[6,64,128]{2,0,1:T(8,128)} %scatter_fusion.1), calls=%async_computation.1 | async-start | bytes 524288 | tf_op jit(solution)/shard_map/all_to_all | solution.py:67
  44.1 31.1 %gather_fusion = f32[8192,8]{1,0:T(8,128)} fusion(f32[8,16384]{0,1:T(8,128)} %copy.25, s32[8192]{0:T(1024)S(1)} %fusion.46), kind=kCustom, calls=%fused_computation.clone | custom fusion | bytes 557056 | tf_op jit(solution)/shard_map/jit(_take)/gather | solution.py:91
  75.3 2.8 copy.26
  78.2 0.2 multiply_bitcast_fusion.1
  78.4 2.7 copy.28
  81.1 55.2 %scatter_custom_fusion.2 = f32[2,16384]{0,1:T(8,128)} fusion(s32[8192]{0:T(1024)S(1)} %bitcast.208, f32[8192,2]{1,0:T(8,128)} %copy.28, f32[]{:T(128)} %constant.20.clone.1), kind=kCustom, calls=%fused_computation.8 | custom fusion | flops 16384 | bytes 131584 | tf_op jit(solution)/shard_map/scatter-add | solution.py:96
  136.3 5.2 %copy.29 = f32[2,8,8,256]{3,2,1,0:T(8,128)S(1)} copy(f32[2,8,8,256]{0,3,2,1:T(8,128)} %bitcast.179) | data formatting | bytes 262144 | tf_op jit(solution)/shard_map/reshape | solution.py:97
  141.5 0.3 subtract_subtract_fusion.1
  141.9 3.1 %collective-permute-start.4 = (f32[2,8,1,256]{3,2,1,0:T(1,128)S(1)}, f32[2,8,1,256]{3,2,1,0:T(1,128)S(1)}, u32[]{:S(2)}, u32[]{:S(2)}) collective-permute-start(f32[2,8,1,256]{3,2,1,0:T(1,128)S(1)} %get-tuple-element.33), channel_id=1, source_target_pairs={{0,4},{4,8},{8,12},{12,16},{16,20},{20,24},{24,28},{1,5},{5,9},{9,... | collective-permute-start | bytes 49160 | tf_op jit(solution)/shard_map/ppermute | solution.py:23
  145.0 2.2 collective-permute-start.5
  147.2 3.2 %collective-permute-done.5 = f32[2,8,1,256]{3,2,1,0:T(1,128)S(1)} collective-permute-done((f32[2,8,1,256]{3,2,1,0:T(1,128)S(1)}, f32[2,8,1,256]{3,2,1,0:T(1,128)S(1)}, u32[]{:S(2)}, u32[]{:S(2)}) %collective-permute-start.5) | collective-permute-done | bytes 16416 | tf_op jit(solution)/shard_map/ppermute | solution.py:24
  150.5 3.7 %collective-permute-start.7 = (f32[2,8,10,1]{3,2,1,0:T(8,128)S(1)}, f32[2,8,10,1]{3,2,1,0:T(8,128)S(1)}, u32[]{:S(2)}, u32[]{:S(2)}) collective-permute-start(f32[2,8,10,1]{3,2,1,0:T(8,128)S(1)} %get-tuple-element.11), channel_id=1, source_target_pairs={{1,0},{2,1},{3,2},{5,4},{6,5},{7,6},{9,8},{10,9},{11,10},{13,12},{... | collective-permute-start | bytes 1928 | tf_op jit(solution)/shard_map/ppermute | solution.py:24
  154.3 3.3 %collective-permute-start.6 = (f32[2,8,10,1]{3,2,1,0:T(8,128)S(1)}, f32[2,8,10,1]{3,2,1,0:T(8,128)S(1)}, u32[]{:S(2)}, u32[]{:S(2)}) collective-permute-start(f32[2,8,10,1]{3,2,1,0:T(8,128)S(1)} %get-tuple-element.12), channel_id=1, source_target_pairs={{0,1},{1,2},{2,3},{4,5},{5,6},{6,7},{8,9},{9,10},{10,11},{12,13},{... | collective-permute-start | bytes 1928 | tf_op jit(solution)/shard_map/ppermute | solution.py:23
  157.5 0.7 collective-permute-done.7
  158.3 1.2 collective-permute-done.6
  159.5 0.3 select_maximum_fusion.8
  159.8 0.3 fusion.11
  160.3 1.9 collective-permute-start.8
  162.2 3.4 %collective-permute-start.9 = (f32[2,8,1,256]{3,2,1,0:T(1,128)S(1)}, f32[2,8,1,256]{3,2,1,0:T(1,128)S(1)}, u32[]{:S(2)}, u32[]{:S(2)}) collective-permute-start(f32[2,8,1,256]{3,2,1,0:T(1,128)S(1)} %get-tuple-element.32), channel_id=1, source_target_pairs={{4,0},{8,4},{12,8},{16,12},{20,16},{24,20},{28,24},{5,1},{9,5},{13... | collective-permute-start | bytes 49160 | tf_op jit(solution)/shard_map/ppermute | solution.py:24
  165.6 2.0 collective-permute-done.9
  167.7 5.7 %collective-permute-start.10 = (f32[2,8,10,1]{3,2,1,0:T(8,128)S(1)}, f32[2,8,10,1]{3,2,1,0:T(8,128)S(1)}, u32[]{:S(2)}, u32[]{:S(2)}) collective-permute-start(f32[2,8,10,1]{3,2,1,0:T(8,128)S(1)} %get-tuple-element.9), channel_id=1, source_target_pairs={{0,1},{1,2},{2,3},{4,5},{5,6},{6,7},{8,9},{9,10},{10,11},{12,13},{... | collective-permute-start | bytes 1928 | tf_op jit(solution)/shard_map/ppermute | solution.py:23
  173.5 2.1 collective-permute-start.11
  175.6 4.1 %collective-permute-done.11 = f32[2,8,10,1]{3,2,1,0:T(8,128)S(1)} collective-permute-done((f32[2,8,10,1]{3,2,1,0:T(8,128)S(1)}, f32[2,8,10,1]{3,2,1,0:T(8,128)S(1)}, u32[]{:S(2)}, u32[]{:S(2)}) %collective-permute-start.11) | collective-permute-done | bytes 672 | tf_op jit(solution)/shard_map/ppermute | solution.py:24
  179.8 0.3 select_maximum_fusion.4
  180.1 0.3 subtract_bitcast_fusion.1
  180.5 5.3 %copy.30 = f32[8,16384]{0,1:T(8,128)} copy(f32[8,16384]{1,0:T(8,128)S(1)} %reshape.135) | data formatting | bytes 1048576 | tf_op jit(solution)/shard_map/reshape | solution.py:90
  185.8 31.1 %gather_fusion.1 = f32[8192,8]{1,0:T(8,128)} fusion(f32[8,16384]{0,1:T(8,128)} %copy.30, s32[8192]{0:T(1024)S(1)} %fusion.46), kind=kCustom, calls=%fused_computation.1.clone | custom fusion | bytes 557056 | tf_op jit(solution)/shard_map/jit(_take)/gather | solution.py:91
  216.9 2.8 copy.31
  219.7 0.2 multiply_bitcast_fusion
  219.9 2.7 copy.32
  222.6 55.2 %scatter_custom_fusion.3 = f32[2,16384]{0,1:T(8,128)} fusion(s32[8192]{0:T(1024)S(1)} %bitcast.209, f32[8192,2]{1,0:T(8,128)} %copy.32, f32[]{:T(128)} %constant.20.clone.1), kind=kCustom, calls=%fused_computation.6 | custom fusion | flops 16384 | bytes 131584 | tf_op jit(solution)/shard_map/scatter-add | solution.py:96
  277.8 5.2 %copy.33 = f32[2,8,8,256]{3,2,1,0:T(8,128)S(1)} copy(f32[2,8,8,256]{0,3,2,1:T(8,128)} %bitcast.178) | data formatting | bytes 262144 | tf_op jit(solution)/shard_map/reshape | solution.py:97
  283.0 0.3 subtract_subtract_fusion
  283.4 2.3 collective-permute-start.12
  285.7 3.0 collective-permute-start.13
  288.7 2.4 collective-permute-done.13
  291.2 1.9 collective-permute-start.15
  293.1 3.6 %collective-permute-start.14 = (f32[2,8,10,1]{3,2,1,0:T(8,128)S(1)}, f32[2,8,10,1]{3,2,1,0:T(8,128)S(1)}, u32[]{:S(2)}, u32[]{:S(2)}) collective-permute-start(f32[2,8,10,1]{3,2,1,0:T(8,128)S(1)} %get-tuple-element.8), channel_id=1, source_target_pairs={{0,1},{1,2},{2,3},{4,5},{5,6},{6,7},{8,9},{9,10},{10,11},{12,13},{... | collective-permute-start | bytes 1928 | tf_op jit(solution)/shard_map/ppermute | solution.py:23
  296.8 0.7 collective-permute-done.15
  297.5 1.2 collective-permute-done.14
  298.7 0.3 select_maximum_fusion
  299.0 0.3 fusion.6
  299.4 0.7 fusion.18
  (54 shorter events, 1.6 us)
Async XLA Ops:
  0.6 20.5 %collective-permute-start.1 = (f32[2,8,1,256]{3,2,1,0:T(1,128)S(1)}, f32[2,8,1,256]{3,2,1,0:T(1,128)S(1)}, u32[]{:S(2)}, u32[]{:S(2)}) collective-permute-start(f32[2,8,1,256]{3,2,1,0:T(1,128)S(1)} %broadcast.87), channel_id=1, source_target_pairs={{4,0},{8,4},{12,8},{16,12},{20,16},{24,20},{28,24},{5,1},{9,5},{13... | collective-permute-start | bytes 49160 | tf_op jit(solution)/shard_map/ppermute | solution.py:24
  2.6 18.5 %collective-permute-start = (f32[2,8,1,256]{3,2,1,0:T(1,128)S(1)}, f32[2,8,1,256]{3,2,1,0:T(1,128)S(1)}, u32[]{:S(2)}, u32[]{:S(2)}) collective-permute-start(f32[2,8,1,256]{3,2,1,0:T(1,128)S(1)} %broadcast.87), channel_id=1, source_target_pairs={{0,4},{4,8},{8,12},{12,16},{16,20},{20,24},{24,28},{1,5},{5,9},{9,... | collective-permute-start | bytes 49160 | tf_op jit(solution)/shard_map/ppermute | solution.py:23
  14.2 23.7 %all-to-all-start = ((s32[2,64,128]{2,0,1:T(2,128)}), s32[2,64,128]{2,0,1:T(2,128)S(1)}, u32[]{:S(2)}, u32[]{:S(2)}) async-start(s32[2,64,128]{2,0,1:T(2,128)} %scatter_fusion), calls=%async_computation | async-start | bytes 131072 | tf_op jit(solution)/shard_map/all_to_all | solution.py:68
  21.3 10.4 %collective-permute-start.2 = (f32[2,8,10,1]{3,2,1,0:T(8,128)S(1)}, f32[2,8,10,1]{3,2,1,0:T(8,128)S(1)}, u32[]{:S(2)}, u32[]{:S(2)}) collective-permute-start(f32[2,8,10,1]{3,2,1,0:T(8,128)S(1)} %get-tuple-element.17), channel_id=1, source_target_pairs={{0,1},{1,2},{2,3},{4,5},{5,6},{6,7},{8,9},{9,10},{10,11},{12,13},{... | collective-permute-start | bytes 1928 | tf_op jit(solution)/shard_map/ppermute | solution.py:23
  24.6 7.1 %collective-permute-start.3 = (f32[2,8,10,1]{3,2,1,0:T(8,128)S(1)}, f32[2,8,10,1]{3,2,1,0:T(8,128)S(1)}, u32[]{:S(2)}, u32[]{:S(2)}) collective-permute-start(f32[2,8,10,1]{3,2,1,0:T(8,128)S(1)} %get-tuple-element.18), channel_id=1, source_target_pairs={{1,0},{2,1},{3,2},{5,4},{6,5},{7,6},{9,8},{10,9},{11,10},{13,12},{... | collective-permute-start | bytes 1928 | tf_op jit(solution)/shard_map/ppermute | solution.py:24
  37.9 40.2 %all-to-all-start.1 = ((f32[6,64,128]{2,0,1:T(8,128)}), f32[6,64,128]{2,0,1:T(8,128)S(1)}, u32[]{:S(2)}, u32[]{:S(2)}) async-start(f32[6,64,128]{2,0,1:T(8,128)} %scatter_fusion.1), calls=%async_computation.1 | async-start | bytes 524288 | tf_op jit(solution)/shard_map/all_to_all | solution.py:67
  81.1 60.4 %copy-start.2 = (f32[2,8,8,256]{3,2,1,0:T(8,128)S(1)}, f32[2,8,8,256]{3,2,1,0:T(8,128)}, u32[]{:S(2)}) copy-start(f32[2,8,8,256]{3,2,1,0:T(8,128)} %param.10) | copy-start | bytes 393220
  81.1 60.7 %copy-start = (f32[8,8,256]{2,1,0:T(8,128)S(1)}, f32[8,8,256]{2,1,0:T(8,128)}, u32[]{:S(2)}) copy-start(f32[8,8,256]{2,1,0:T(8,128)} %param.11) | copy-start | bytes 196612
  141.9 5.3 %collective-permute-start.4 = (f32[2,8,1,256]{3,2,1,0:T(1,128)S(1)}, f32[2,8,1,256]{3,2,1,0:T(1,128)S(1)}, u32[]{:S(2)}, u32[]{:S(2)}) collective-permute-start(f32[2,8,1,256]{3,2,1,0:T(1,128)S(1)} %get-tuple-element.33), channel_id=1, source_target_pairs={{0,4},{4,8},{8,12},{12,16},{16,20},{20,24},{24,28},{1,5},{5,9},{9,... | collective-permute-start | bytes 49160 | tf_op jit(solution)/shard_map/ppermute | solution.py:23
  145.0 5.4 %collective-permute-start.5 = (f32[2,8,1,256]{3,2,1,0:T(1,128)S(1)}, f32[2,8,1,256]{3,2,1,0:T(1,128)S(1)}, u32[]{:S(2)}, u32[]{:S(2)}) collective-permute-start(f32[2,8,1,256]{3,2,1,0:T(1,128)S(1)} %get-tuple-element.34), channel_id=1, source_target_pairs={{4,0},{8,4},{12,8},{16,12},{20,16},{24,20},{28,24},{5,1},{9,5},{13... | collective-permute-start | bytes 49160 | tf_op jit(solution)/shard_map/ppermute | solution.py:24
  150.5 7.7 %collective-permute-start.7 = (f32[2,8,10,1]{3,2,1,0:T(8,128)S(1)}, f32[2,8,10,1]{3,2,1,0:T(8,128)S(1)}, u32[]{:S(2)}, u32[]{:S(2)}) collective-permute-start(f32[2,8,10,1]{3,2,1,0:T(8,128)S(1)} %get-tuple-element.11), channel_id=1, source_target_pairs={{1,0},{2,1},{3,2},{5,4},{6,5},{7,6},{9,8},{10,9},{11,10},{13,12},{... | collective-permute-start | bytes 1928 | tf_op jit(solution)/shard_map/ppermute | solution.py:24
  154.3 5.2 %collective-permute-start.6 = (f32[2,8,10,1]{3,2,1,0:T(8,128)S(1)}, f32[2,8,10,1]{3,2,1,0:T(8,128)S(1)}, u32[]{:S(2)}, u32[]{:S(2)}) collective-permute-start(f32[2,8,10,1]{3,2,1,0:T(8,128)S(1)} %get-tuple-element.12), channel_id=1, source_target_pairs={{0,1},{1,2},{2,3},{4,5},{5,6},{6,7},{8,9},{9,10},{10,11},{12,13},{... | collective-permute-start | bytes 1928 | tf_op jit(solution)/shard_map/ppermute | solution.py:23
  160.3 5.3 %collective-permute-start.8 = (f32[2,8,1,256]{3,2,1,0:T(1,128)S(1)}, f32[2,8,1,256]{3,2,1,0:T(1,128)S(1)}, u32[]{:S(2)}, u32[]{:S(2)}) collective-permute-start(f32[2,8,1,256]{3,2,1,0:T(1,128)S(1)} %get-tuple-element.31), channel_id=1, source_target_pairs={{0,4},{4,8},{8,12},{12,16},{16,20},{20,24},{24,28},{1,5},{5,9},{9,... | collective-permute-start | bytes 49160 | tf_op jit(solution)/shard_map/ppermute | solution.py:23
  162.2 5.4 %collective-permute-start.9 = (f32[2,8,1,256]{3,2,1,0:T(1,128)S(1)}, f32[2,8,1,256]{3,2,1,0:T(1,128)S(1)}, u32[]{:S(2)}, u32[]{:S(2)}) collective-permute-start(f32[2,8,1,256]{3,2,1,0:T(1,128)S(1)} %get-tuple-element.32), channel_id=1, source_target_pairs={{4,0},{8,4},{12,8},{16,12},{20,16},{24,20},{28,24},{5,1},{9,5},{13... | collective-permute-start | bytes 49160 | tf_op jit(solution)/shard_map/ppermute | solution.py:24
  167.7 7.9 %collective-permute-start.10 = (f32[2,8,10,1]{3,2,1,0:T(8,128)S(1)}, f32[2,8,10,1]{3,2,1,0:T(8,128)S(1)}, u32[]{:S(2)}, u32[]{:S(2)}) collective-permute-start(f32[2,8,10,1]{3,2,1,0:T(8,128)S(1)} %get-tuple-element.9), channel_id=1, source_target_pairs={{0,1},{1,2},{2,3},{4,5},{5,6},{6,7},{8,9},{9,10},{10,11},{12,13},{... | collective-permute-start | bytes 1928 | tf_op jit(solution)/shard_map/ppermute | solution.py:23
  173.5 6.3 %collective-permute-start.11 = (f32[2,8,10,1]{3,2,1,0:T(8,128)S(1)}, f32[2,8,10,1]{3,2,1,0:T(8,128)S(1)}, u32[]{:S(2)}, u32[]{:S(2)}) collective-permute-start(f32[2,8,10,1]{3,2,1,0:T(8,128)S(1)} %get-tuple-element.10), channel_id=1, source_target_pairs={{1,0},{2,1},{3,2},{5,4},{6,5},{7,6},{9,8},{10,9},{11,10},{13,12},{... | collective-permute-start | bytes 1928 | tf_op jit(solution)/shard_map/ppermute | solution.py:24
  283.3 16.9 %copy-start.1 = (f32[2,8,8,256]{3,2,1,0:T(8,128)}, f32[2,8,8,256]{3,2,1,0:T(8,128)S(1)}, u32[]{:S(2)}) copy-start(f32[2,8,8,256]{3,2,1,0:T(8,128)S(1)} %subtract_subtract_fusion) | copy-start | bytes 393220
  283.4 5.3 %collective-permute-start.12 = (f32[2,8,1,256]{3,2,1,0:T(1,128)S(1)}, f32[2,8,1,256]{3,2,1,0:T(1,128)S(1)}, u32[]{:S(2)}, u32[]{:S(2)}) collective-permute-start(f32[2,8,1,256]{3,2,1,0:T(1,128)S(1)} %get-tuple-element.29), channel_id=1, source_target_pairs={{0,4},{4,8},{8,12},{12,16},{16,20},{20,24},{24,28},{1,5},{5,9},{9,... | collective-permute-start | bytes 49160 | tf_op jit(solution)/shard_map/ppermute | solution.py:23
  285.7 5.4 %collective-permute-start.13 = (f32[2,8,1,256]{3,2,1,0:T(1,128)S(1)}, f32[2,8,1,256]{3,2,1,0:T(1,128)S(1)}, u32[]{:S(2)}, u32[]{:S(2)}) collective-permute-start(f32[2,8,1,256]{3,2,1,0:T(1,128)S(1)} %get-tuple-element.30), channel_id=1, source_target_pairs={{4,0},{8,4},{12,8},{16,12},{20,16},{24,20},{28,24},{5,1},{9,5},{13... | collective-permute-start | bytes 49160 | tf_op jit(solution)/shard_map/ppermute | solution.py:24
  291.2 6.3 %collective-permute-start.15 = (f32[2,8,10,1]{3,2,1,0:T(8,128)S(1)}, f32[2,8,10,1]{3,2,1,0:T(8,128)S(1)}, u32[]{:S(2)}, u32[]{:S(2)}) collective-permute-start(f32[2,8,10,1]{3,2,1,0:T(8,128)S(1)} %get-tuple-element.7), channel_id=1, source_target_pairs={{1,0},{2,1},{3,2},{5,4},{6,5},{7,6},{9,8},{10,9},{11,10},{13,12},{... | collective-permute-start | bytes 1928 | tf_op jit(solution)/shard_map/ppermute | solution.py:24
  293.1 5.6 %collective-permute-start.14 = (f32[2,8,10,1]{3,2,1,0:T(8,128)S(1)}, f32[2,8,10,1]{3,2,1,0:T(8,128)S(1)}, u32[]{:S(2)}, u32[]{:S(2)}) collective-permute-start(f32[2,8,10,1]{3,2,1,0:T(8,128)S(1)} %get-tuple-element.8), channel_id=1, source_target_pairs={{0,1},{1,2},{2,3},{4,5},{5,6},{6,7},{8,9},{9,10},{10,11},{12,13},{... | collective-permute-start | bytes 1928 | tf_op jit(solution)/shard_map/ppermute | solution.py:23
where the time goes:
time: 302 us; the launch traced here: 300 us
  other arithmetic  120 us (40%)
  local copies, waits for them, and re-layouts  104 us (34%)
  starting transfers between devices  59.8 us (20%)
  waiting for transfers between devices  15.6 us (5%)
    scatter-add x2, other arithmetic, per_device(): jnp.zeros((2, planes * per_plane), jnp.float32).at[:, cells].add(penalty)  110 us
    gather x4, local copies, waits for them, and re-layouts, per_device(): picked = jnp.take(features, cells, axis=1).reshape(4, 2, -1)  67.8 us
    ppermute x8, starting transfers between devices, with_halo(): before = lax.ppermute(last, axis, up)  27.6 us
    ppermute x8, starting transfers between devices, with_halo(): after = lax.ppermute(first, axis, down)  20.1 us
    ppermute x8, waiting for transfers between devices, with_halo(): after = lax.ppermute(first, axis, down)  13.1 us
    reshape x4, local copies, waits for them, and re-layouts, per_device(): features = jnp.stack([center, diff_z, diff_x, diff_y]).reshape(8, -1)  10.8 us
    reshape x2, local copies, waits for them, and re-layouts, per_device(): residual = rhs_field - image - surface.reshape(rhs_field.shape)  10.4 us
    all_to_all x1, starting transfers between devices, per_device(): lax.all_to_all(float_send, ('gx', 'gy'), split_axis=1, concat_axis=1, til...  6.13 us
  transfers between devices with their start and end apart: 18, of which 8 were waited for; matrix products, arithmetic and copies ran while one was open for 18% of the time, Pallas kernels for 0%

commit v1 on v0

v1 whole, which is shorter than its diff:
```python
import functools

import jax
import jax.numpy as jnp
from jax import lax
from jax.experimental import pallas as pl
from jax.experimental.pallas import tpu as pltpu
from jax.sharding import PartitionSpec as P

CAP = 2
K_SQUARED = 0.25
BETA = 0.5
OMEGA = 0.8
TAU = 1.0
FIELDS = 8
PARTS = 11
GROUP = 8
ROUNDS = 3
MESH = pl.DeviceIdType.MESH
F32 = jnp.float32
BF16 = jnp.bfloat16


def iota(shape, dim):
    return lax.broadcasted_iota(jnp.int32, shape, dim)


def kernel(
    n_gx, n_gy,
    rhs_ref, perm_ref, dist_ref, normal_ref, inc_ref, cell_ref, mask_ref, owner_ref,
    sol_ref, res_ref,
    send, recv, left, right, acc, row_send, row_recv, col_send, col_recv,
    block_out, block_in, halo_out, halo_in,
):
    gx, gy = lax.axis_index("gx"), lax.axis_index("gy")
    n = n_gx * n_gy
    me = gx * n_gy + gy
    blocks, points = cell_ref.shape
    planes, rows, cols = perm_ref.shape
    lines = planes * rows

    def peer(k):
        to = lax.rem(me + k, n)
        return to, (lax.div(to, n_gy), lax.rem(to, n_gy))

    barrier = pltpu.get_barrier_semaphore()

    def greet(k, carry):
        pl.semaphore_signal(barrier, inc=1, device_id=peer(k)[1], device_id_type=MESH)
        return carry

    lax.fori_loop(1, n, greet, 0)

    weight = TAU * mask_ref[...].astype(F32)
    half = weight * dist_ref[...] * 0.5
    data = jnp.concatenate(
        [
            cell_ref[...].astype(F32), weight,
            half * normal_ref[0], half * normal_ref[1], half * normal_ref[2],
            weight * inc_ref[0], weight * inc_ref[1],
            jnp.zeros((blocks, points), F32),
        ],
        axis=0,
    )
    wide = FIELDS * blocks
    lane_no = iota((blocks, wide), 1)
    lane_block = lane_no % blocks
    row_block = iota((blocks, wide), 0)
    owner = jnp.broadcast_to(owner_ref[...].astype(F32), (blocks, wide))
    owner_of = jnp.sum(jnp.where(row_block == lane_block, owner, 0.0), axis=0, keepdims=True)
    earlier = (owner == owner_of) & (row_block < lane_block)
    rank = jnp.sum(jnp.where(earlier, 1.0, 0.0), axis=0, keepdims=True)
    field_no = (iota((1, wide), 1) // blocks).astype(F32)
    target = (owner_of * CAP + rank) * FIELDS + field_no
    slots = n * CAP * FIELDS
    chosen = jnp.where(iota((slots, wide), 0).astype(F32) == target, 1.0, 0.0).astype(BF16)
    high = data.astype(BF16)
    rest = data - high.astype(F32)
    middle = rest.astype(BF16)
    low = (rest - middle.astype(F32)).astype(BF16)
    placed = jnp.dot(chosen, high, preferred_element_type=F32)
    placed = placed + jnp.dot(chosen, middle, preferred_element_type=F32)
    placed = placed + jnp.dot(chosen, low, preferred_element_type=F32)
    send[...] = placed.reshape(n, CAP * FIELDS, points)

    pl.semaphore_wait(barrier, n - 1)

    def block_copy(k):
        to, where = peer(k)
        return pltpu.make_async_remote_copy(
            src_ref=send.at[to], dst_ref=recv.at[k],
            send_sem=block_out.at[k], recv_sem=block_in.at[k],
            device_id=where, device_id_type=MESH,
        )

    def start_block(k, carry):
        block_copy(k).start()
        return carry

    lax.fori_loop(1, n, start_block, 0)
    recv[0] = send[me]

    @pl.when(gx == 0)
    def _():
        row_recv[:, 0] = jnp.zeros((ROUNDS, 2 * planes, cols), F32)

    @pl.when(gx == n_gx - 1)
    def _():
        row_recv[:, 1] = jnp.zeros((ROUNDS, 2 * planes, cols), F32)

    @pl.when(gy == 0)
    def _():
        col_recv[:, 0] = jnp.zeros((ROUNDS, 8, 2 * lines), F32)

    @pl.when(gy == n_gy - 1)
    def _():
        col_recv[:, 1] = jnp.zeros((ROUNDS, 8, 2 * lines), F32)

    perm = perm_ref[...]
    diag = 6.0 - K_SQUARED * perm
    shift = BETA * K_SQUARED * perm
    denom = diag * diag + shift * shift
    inv_real = diag / denom
    inv_imag = -shift / denom
    both_diag = jnp.concatenate([diag, diag], axis=0)

    acc[...] = jnp.zeros(acc.shape, F32)
    line_no = iota((lines, points), 0).astype(F32)
    col_no = iota((cols, points), 0).astype(F32)

    def gather_group(g, carry):
        for j in range(GROUP):
            k = g * GROUP + j

            @pl.when(k > 0)
            def _():
                block_copy(k).wait_recv()

        for j in range(GROUP):
            for r in range(CAP):
                tile = recv[g * GROUP + j, r * FIELDS:(r + 1) * FIELDS, :]
                at = slice((j * CAP + r) * points, (j * CAP + r + 1) * points)
                cell = tile[0:1]
                line = jnp.floor(cell * (1.0 / cols))
                column = cell - line * cols
                right[:, at] = jnp.where(col_no == column, 1.0, 0.0).astype(BF16)
                here = line_no == line
                left[0:lines, at] = jnp.where(here, tile[1:2], 0.0).astype(BF16)
                upper = tile.astype(BF16).astype(F32)
                lower = tile - upper
                for f in range(5):
                    for p, part in enumerate((upper, lower)):
                        top = (1 + 2 * f + p) * lines
                        value = jnp.where(here, part[2 + f:3 + f], 0.0)
                        left[top:top + lines, at] = value.astype(BF16)
        acc[...] += lax.dot_general(
            left[...], right[...], (((1,), (1,)), ((), ())), preferred_element_type=F32
        )
        return carry

    lax.fori_loop(0, n // GROUP, gather_group, 0)

    def summed(f):
        top = (1 + 2 * f) * lines
        both = acc[top:top + lines, :] + acc[top + lines:top + 2 * lines, :]
        return both.reshape(planes, rows, cols)

    def twice(x):
        return jnp.concatenate([x, x], axis=0)

    def precond(vec):
        real, imag = vec[:planes], vec[planes:]
        return jnp.concatenate(
            [real * inv_real - imag * inv_imag, real * inv_imag + imag * inv_real], axis=0
        )

    def halo_copies(step):
        out = []
        for side, (there, dx, dy) in enumerate(
            ((gx < n_gx - 1, 1, 0), (gx > 0, -1, 0), (gy < n_gy - 1, 0, 1), (gy > 0, 0, -1))
        ):
            source, sink = (row_send, row_recv) if side < 2 else (col_send, col_recv)
            out.append((there, pltpu.make_async_remote_copy(
                src_ref=source.at[step, side % 2], dst_ref=sink.at[step, side % 2],
                send_sem=halo_out.at[step, side], recv_sem=halo_in.at[step, side],
                device_id=(gx + dx, gy + dy), device_id_type=MESH,
            )))
        return out

    full = (2 * planes, rows, cols)
    row_at, col_at = iota(full, 1), iota(full, 2)

    def beside(step, v):
        flat = v.reshape(2 * lines, cols)
        row_send[step, 0] = v[:, rows - 1, :]
        row_send[step, 1] = v[:, 0, :]
        col_send[step, 0] = jnp.transpose(flat[:, cols - 128:])[120:128]
        col_send[step, 1] = jnp.transpose(flat[:, :128])[0:8]
        copies = halo_copies(step)
        for there, copy in copies:
            pl.when(there)(copy.start)
        zero = jnp.zeros((1, rows, cols), F32)
        z_next = jnp.concatenate([v[1:planes], zero, v[planes + 1:], zero], axis=0)
        z_last = jnp.concatenate([zero, v[:planes - 1], zero, v[planes:-1]], axis=0)
        x_next = pltpu.roll(v, rows - 1, 1)
        x_last = pltpu.roll(v, 1, 1)
        y_next = pltpu.roll(v, cols - 1, 2)
        y_last = pltpu.roll(v, 1, 2)
        for side, (there, copy) in enumerate(copies):
            comes = copies[side ^ 1][0]
            pl.when(comes)(copy.wait_recv)
            pl.when(there)(copy.wait_send)
        x_last = jnp.where(row_at == 0, row_recv[step, 0][:, None, :], x_last)
        x_next = jnp.where(row_at == rows - 1, row_recv[step, 1][:, None, :], x_next)

        def edge(row):
            column = jnp.transpose(jnp.broadcast_to(row, (2 * lines, 2 * lines)))
            return jnp.concatenate([column] * (cols // (2 * lines)), axis=1).reshape(full)

        y_last = jnp.where(col_at == 0, edge(col_recv[step, 0, 7:8, :]), y_last)
        y_next = jnp.where(col_at == cols - 1, edge(col_recv[step, 1, 0:1, :]), y_next)
        return z_next, z_last, x_next, x_last, y_next, y_last

    def helm(v, around):
        z_next, z_last, x_next, x_last, y_next, y_last = around
        return both_diag * v - (z_next + z_last + x_next + x_last + y_next + y_last)

    def sweep(step, z, residual):
        image = helm(z, beside(step, z))
        real = image[:planes] - shift * z[planes:]
        imag = image[planes:] + shift * z[:planes]
        return z + OMEGA * precond(residual - jnp.concatenate([real, imag], axis=0))

    source = rhs_ref[...] - jnp.concatenate([summed(3), summed(4)], axis=0)
    solution = sweep(0, OMEGA * precond(source), source)
    around = beside(1, solution)
    z_next, z_last, x_next, x_last, y_next, y_last = around
    surface = twice(acc[0:lines, :].reshape(planes, rows, cols)) * solution
    surface = surface + twice(summed(0)) * (z_next - z_last)
    surface = surface + twice(summed(1)) * (x_next - x_last)
    surface = surface + twice(summed(2)) * (y_next - y_last)
    residual = source - helm(solution, around) - surface
    res_ref[...] = residual
    sol_ref[...] = solution + sweep(2, OMEGA * precond(residual), residual)

    def finish_block(k, carry):
        block_copy(k).wait_send()
        return carry

    lax.fori_loop(1, n, finish_block, 0)


def per_device(
    n_gx, n_gy,
    rhs_field, permittivity, surf_dist, surf_normal, surf_inc, surf_cell, surf_mask, surf_owner,
):
    planes, rows, cols = permittivity.shape
    points = surf_cell.shape[1]
    n = n_gx * n_gy
    lines = planes * rows
    field = jax.ShapeDtypeStruct((2 * planes, rows, cols), F32)
    vmem = pl.BlockSpec(memory_space=pltpu.VMEM)
    deep = GROUP * CAP * points
    sol, res = pl.pallas_call(
        functools.partial(kernel, n_gx, n_gy),
        out_shape=(field, field),
        in_specs=[vmem] * 8,
        out_specs=(vmem, vmem),
        scratch_shapes=[
            pltpu.VMEM((n, CAP * FIELDS, points), F32),
            pltpu.VMEM((n, CAP * FIELDS, points), F32),
            pltpu.VMEM((PARTS * lines, deep), BF16),
            pltpu.VMEM((cols, deep), BF16),
            pltpu.VMEM((PARTS * lines, cols), F32),
            pltpu.VMEM((ROUNDS, 2, 2 * planes, cols), F32),
            pltpu.VMEM((ROUNDS, 2, 2 * planes, cols), F32),
            pltpu.VMEM((ROUNDS, 2, 8, 2 * lines), F32),
            pltpu.VMEM((ROUNDS, 2, 8, 2 * lines), F32),
            pltpu.SemaphoreType.DMA((n,)),
            pltpu.SemaphoreType.DMA((n,)),
            pltpu.SemaphoreType.DMA((ROUNDS, 4)),
            pltpu.SemaphoreType.DMA((ROUNDS, 4)),
        ],
        compiler_params=pltpu.CompilerParams(
            collective_id=0, has_side_effects=True, vmem_limit_bytes=48 * 1024 * 1024
        ),
    )(
        rhs_field.reshape(field.shape), permittivity, surf_dist, surf_normal, surf_inc,
        surf_cell, surf_mask, surf_owner,
    )
    return sol.reshape(rhs_field.shape), res.reshape(rhs_field.shape)


def solution(mesh):
    placed = (
        P(None, None, "gx", "gy"),
        P(None, "gx", "gy"),
        P(("gx", "gy"), None),
        P(None, ("gx", "gy"), None),
        P(None, ("gx", "gy"), None),
        P(("gx", "gy"), None),
        P(("gx", "gy"), None),
        P(("gx", "gy"), None),
    )
    return jax.shard_map(
        functools.partial(per_device, mesh.shape["gx"], mesh.shape["gy"]),
        mesh=mesh,
        in_specs=placed,
        out_specs=(P(None, None, "gx", "gy"), P(None, None, "gx", "gy")),
        check_vma=False,
    )
```

time: 302 us -> 34.7 us (0.11)
  the two profiles are of different devices: /device:TPU:3 before, /device:TPU:0 now
where the time goes in v1:
time: 34.7 us; the launch traced here: 34.3 us
  Pallas kernels  26.8 us (77%)
  local copies, waits for them, and re-layouts  6.77 us (20%)
  between operations  0.66 us (2%)
    pallas_call x1, Pallas kernels, per_device(): pl.pallas_call(functools.partial(kernel, n_gx, n_gy), out_shape=(field, f...  26.8 us
    unnamed x19, local copies, waits for them, and re-layouts  6.77 us

profile of v1, /device:TPU:0, one launch (start us, length us, event | category | flops | bytes accessed | tf_op | source)
XLA Modules:
  0.0 34.3 jit_solution(6877878295510635380)
XLA Ops:
  0.6 0.0 copy-start.7
  0.6 0.0 copy-start.4
  0.6 0.6 %copy-done.7 = s32[32,1]{0,1:T(1,128)S(1)} copy-done((s32[32,1]{0,1:T(1,128)S(1)}, s32[32,1]{0,1:T(1,128)}, u32[]{:S(2)}) %copy-start.7) | copy-done | bytes 152
  1.3 0.1 copy.10.owner_ref
  1.4 0.0 copy-done.4
  1.4 0.0 copy-start
  1.4 0.9 %copy-done = f32[2,8,8,256]{3,2,1,0:T(8,128)S(1)} copy-done((f32[2,8,8,256]{3,2,1,0:T(8,128)S(1)}, f32[2,8,8,256]{3,2,1,0:T(8,128)}, u32[]{:S(2)}) %copy-start) | copy-done | bytes 131096
  2.3 0.0 copy-start.1
  2.3 0.8 %copy-done.1 = f32[8,8,256]{2,1,0:T(8,128)S(1)} copy-done((f32[8,8,256]{2,1,0:T(8,128)S(1)}, f32[8,8,256]{2,1,0:T(8,128)}, u32[]{:S(2)}) %copy-start.1) | copy-done | bytes 65560
  3.1 0.0 copy-start.2
  3.1 0.8 %copy-done.2 = f32[3,32,128]{2,1,0:T(8,128)S(1)} copy-done((f32[3,32,128]{2,1,0:T(8,128)S(1)}, f32[3,32,128]{2,1,0:T(8,128)}, u32[]{:S(2)}) %copy-start.2) | copy-done | bytes 49176
  3.9 0.0 copy-start.3
  3.9 0.8 %copy-done.3 = f32[2,32,128]{2,1,0:T(8,128)S(1)} copy-done((f32[2,32,128]{2,1,0:T(8,128)S(1)}, f32[2,32,128]{2,1,0:T(8,128)}, u32[]{:S(2)}) %copy-start.3) | copy-done | bytes 32792
  4.7 0.0 copy-start.5
  4.7 0.7 %copy-done.5 = s32[32,128]{1,0:T(8,128)S(1)} copy-done((s32[32,128]{1,0:T(8,128)S(1)}, s32[32,128]{1,0:T(8,128)}, u32[]{:S(2)}) %copy-start.5) | copy-done | bytes 16408
  5.4 0.0 copy-start.6
  5.4 0.7 %copy-done.6 = s32[32,128]{1,0:T(8,128)S(1)} copy-done((s32[32,128]{1,0:T(8,128)S(1)}, s32[32,128]{1,0:T(8,128)}, u32[]{:S(2)}) %copy-start.6) | copy-done | bytes 16408
  6.1 26.8 %shard_map.95 = (f32[16,8,256]{2,1,0:T(8,128)S(1)}, f32[16,8,256]{2,1,0:T(8,128)S(1)}) custom-call(f32[16,8,256]{2,1,0:T(8,128)S(1)} %bitcast.3, f32[8,8,256]{2,1,0:T(8,128)S(1)} %copy-done.1, f32[32,128]{1,0:T(8,128)S(1)} %copy-done.4, f32[3,32,128]{2,1,0:T(8,128)S(1)} %copy-done.2, f32[2,32,128]{2,1,0:T(8,128)S(1)} %copy-done.3, s32[32,128]{1,0:T(8,128)S(1)} %copy-done.5, ...), custom_call_target="tpu_custom_call" | custom-call | tf_op jit(solution)/shard_map/pallas_call | solution.py:264
  33.0 0.7 %copy.13 = f32[2,8,8,256]{3,2,1,0:T(8,128)} copy(f32[2,8,8,256]{3,2,1,0:T(8,128)S(1)} %bitcast.5) | data formatting | bytes 262144
  33.6 0.7 %copy.14 = f32[2,8,8,256]{3,2,1,0:T(8,128)} copy(f32[2,8,8,256]{3,2,1,0:T(8,128)S(1)} %bitcast.4) | data formatting | bytes 262144
Async XLA Ops:
  0.6 0.7 %copy-start.7 = (s32[32,1]{0,1:T(1,128)S(1)}, s32[32,1]{0,1:T(1,128)}, u32[]{:S(2)}) copy-start(s32[32,1]{0,1:T(1,128)} %param.15) | copy-start | bytes 388
  0.6 0.7 %copy-start.4 = (f32[32,128]{1,0:T(8,128)S(1)}, f32[32,128]{1,0:T(8,128)}, u32[]{:S(2)}) copy-start(f32[32,128]{1,0:T(8,128)} %dist_ref.1) | copy-start | bytes 49156
  1.4 0.9 %copy-start = (f32[2,8,8,256]{3,2,1,0:T(8,128)S(1)}, f32[2,8,8,256]{3,2,1,0:T(8,128)}, u32[]{:S(2)}) copy-start(f32[2,8,8,256]{3,2,1,0:T(8,128)} %param.8) | copy-start | bytes 393220
  2.3 0.8 %copy-start.1 = (f32[8,8,256]{2,1,0:T(8,128)S(1)}, f32[8,8,256]{2,1,0:T(8,128)}, u32[]{:S(2)}) copy-start(f32[8,8,256]{2,1,0:T(8,128)} %perm_ref.1) | copy-start | bytes 196612
  3.1 0.8 %copy-start.2 = (f32[3,32,128]{2,1,0:T(8,128)S(1)}, f32[3,32,128]{2,1,0:T(8,128)}, u32[]{:S(2)}) copy-start(f32[3,32,128]{2,1,0:T(8,128)} %normal_ref.1) | copy-start | bytes 147460
  3.9 0.8 %copy-start.3 = (f32[2,32,128]{2,1,0:T(8,128)S(1)}, f32[2,32,128]{2,1,0:T(8,128)}, u32[]{:S(2)}) copy-start(f32[2,32,128]{2,1,0:T(8,128)} %inc_ref.1) | copy-start | bytes 98308
  4.7 0.7 %copy-start.5 = (s32[32,128]{1,0:T(8,128)S(1)}, s32[32,128]{1,0:T(8,128)}, u32[]{:S(2)}) copy-start(s32[32,128]{1,0:T(8,128)} %cell_ref.1) | copy-start | bytes 49156
  5.4 0.7 %copy-start.6 = (s32[32,128]{1,0:T(8,128)S(1)}, s32[32,128]{1,0:T(8,128)}, u32[]{:S(2)}) copy-start(s32[32,128]{1,0:T(8,128)} %mask_ref.1) | copy-start | bytes 49156

commit v2 on v1

--- a/solution.py
+++ b/solution.py
@@ -12,7 +12,9 @@
 BETA = 0.5
 OMEGA = 0.8
 TAU = 1.0
-FIELDS = 8
+FIELDS = 7
+SENT = CAP * FIELDS
+ROWS = -(-SENT // 8) * 8
 PARTS = 11
 GROUP = 8
 ROUNDS = 3
@@ -27,10 +29,11 @@
 
 def kernel(
     n_gx, n_gy,
+    rhs_hbm, perm_hbm, dist_hbm, normal_hbm, inc_hbm, cell_hbm, mask_hbm, owner_hbm,
+    sol_hbm, res_hbm,
     rhs_ref, perm_ref, dist_ref, normal_ref, inc_ref, cell_ref, mask_ref, owner_ref,
-    sol_ref, res_ref,
     send, recv, left, right, acc, row_send, row_recv, col_send, col_recv,
-    block_out, block_in, halo_out, halo_in,
+    sol_ref, res_ref, loaded, written, block_out, block_in, halo_out, halo_in,
 ):
     gx, gy = lax.axis_index("gx"), lax.axis_index("gy")
     n = n_gx * n_gy
@@ -50,6 +53,18 @@
         return carry
 
     lax.fori_loop(1, n, greet, 0)
+    loads = [
+        pltpu.make_async_copy(source, sink, loaded.at[i])
+        for i, (source, sink) in enumerate((
+            (owner_hbm, owner_ref), (cell_hbm, cell_ref), (mask_hbm, mask_ref),
+            (dist_hbm, dist_ref), (normal_hbm, normal_ref), (inc_hbm, inc_ref),
+            (perm_hbm, perm_ref), (rhs_hbm, rhs_ref),
+        ))
+    ]
+    for load in loads:
+        load.start()
+    for load in loads[:6]:
+        load.wait()
 
     weight = TAU * mask_ref[...].astype(F32)
     half = weight * dist_ref[...] * 0.5
@@ -58,7 +73,6 @@
             cell_ref[...].astype(F32), weight,
             half * normal_ref[0], half * normal_ref[1], half * normal_ref[2],
             weight * inc_ref[0], weight * inc_ref[1],
-            jnp.zeros((blocks, points), F32),
         ],
         axis=0,
     )
@@ -66,13 +80,15 @@
     lane_no = iota((blocks, wide), 1)
     lane_block = lane_no % blocks
     row_block = iota((blocks, wide), 0)
-    owner = jnp.broadcast_to(owner_ref[...].astype(F32), (blocks, wide))
+    square = (blocks, blocks)
+    owner = jnp.where(iota(square, 0) == iota(square, 1), owner_ref[...].astype(F32), 0.0)
+    owner = jnp.broadcast_to(jnp.sum(owner, axis=1, keepdims=True), (blocks, wide))
     owner_of = jnp.sum(jnp.where(row_block == lane_block, owner, 0.0), axis=0, keepdims=True)
     earlier = (owner == owner_of) & (row_block < lane_block)
     rank = jnp.sum(jnp.where(earlier, 1.0, 0.0), axis=0, keepdims=True)
     field_no = (iota((1, wide), 1) // blocks).astype(F32)
-    target = (owner_of * CAP + rank) * FIELDS + field_no
-    slots = n * CAP * FIELDS
+    target = owner_of * ROWS + rank * FIELDS + field_no
+    slots = n * ROWS
     chosen = jnp.where(iota((slots, wide), 0).astype(F32) == target, 1.0, 0.0).astype(BF16)
     high = data.astype(BF16)
     rest = data - high.astype(F32)
@@ -81,14 +97,14 @@
     placed = jnp.dot(chosen, high, preferred_element_type=F32)
     placed = placed + jnp.dot(chosen, middle, preferred_element_type=F32)
     placed = placed + jnp.dot(chosen, low, preferred_element_type=F32)
-    send[...] = placed.reshape(n, CAP * FIELDS, points)
+    send[...] = placed.reshape(n, ROWS, points)
 
     pl.semaphore_wait(barrier, n - 1)
 
     def block_copy(k):
         to, where = peer(k)
         return pltpu.make_async_remote_copy(
-            src_ref=send.at[to], dst_ref=recv.at[k],
+            src_ref=send.at[to, pl.ds(0, SENT)], dst_ref=recv.at[k, pl.ds(0, SENT)],
             send_sem=block_out.at[k], recv_sem=block_in.at[k],
             device_id=where, device_id_type=MESH,
         )
@@ -99,6 +115,8 @@
 
     lax.fori_loop(1, n, start_block, 0)
     recv[0] = send[me]
+    for load in loads[6:]:
+        load.wait()
 
     @pl.when(gx == 0)
     def _():
@@ -241,13 +259,30 @@
     surface = surface + twice(summed(2)) * (y_next - y_last)
     residual = source - helm(solution, around) - surface
     res_ref[...] = residual
+    res_write = pltpu.make_async_copy(res_ref, res_hbm, written.at[0])
+    res_write.start()
     sol_ref[...] = solution + sweep(2, OMEGA * precond(residual), residual)
+    sol_write = pltpu.make_async_copy(sol_ref, sol_hbm, written.at[1])
+    sol_write.start()
 
     def finish_block(k, carry):
         block_copy(k).wait_send()
         return carry
 
     lax.fori_loop(1, n, finish_block, 0)
+    res_write.wait()
+    sol_write.wait()
+
+
+def write_out(sol_ref, res_ref, sol_hbm, res_hbm, done):
+    copies = (
+        pltpu.make_async_copy(sol_ref, sol_hbm, done.at[0]),
+        pltpu.make_async_copy(res_ref, res_hbm, done.at[1]),
+    )
+    for copy in copies:
+        copy.start()
+    for copy in copies:
+        copy.wait()
 
 
 def per_device(
@@ -259,16 +294,22 @@
     n = n_gx * n_gy
     lines = planes * rows
     field = jax.ShapeDtypeStruct((2 * planes, rows, cols), F32)
-    vmem = pl.BlockSpec(memory_space=pltpu.VMEM)
+    hbm = pl.BlockSpec(memory_space=pltpu.HBM)
+    owner = surf_owner.reshape(1, -1)
+    operands = (
+        rhs_field.reshape(field.shape), permittivity, surf_dist, surf_normal, surf_inc,
+        surf_cell, surf_mask, owner,
+    )
     deep = GROUP * CAP * points
     sol, res = pl.pallas_call(
         functools.partial(kernel, n_gx, n_gy),
         out_shape=(field, field),
-        in_specs=[vmem] * 8,
-        out_specs=(vmem, vmem),
+        in_specs=[hbm] * 8,
+        out_specs=(hbm, hbm),
         scratch_shapes=[
-            pltpu.VMEM((n, CAP * FIELDS, points), F32),
-            pltpu.VMEM((n, CAP * FIELDS, points), F32),
+            *[pltpu.VMEM(x.shape, x.dtype) for x in operands],
+            pltpu.VMEM((n, ROWS, points), F32),
+            pltpu.VMEM((n, ROWS, points), F32),
             pltpu.VMEM((PARTS * lines, deep), BF16),
             pltpu.VMEM((cols, deep), BF16),
             pltpu.VMEM((PARTS * lines, cols), F32),
@@ -276,18 +317,27 @@
             pltpu.VMEM((ROUNDS, 2, 2 * planes, cols), F32),
             pltpu.VMEM((ROUNDS, 2, 8, 2 * lines), F32),
             pltpu.VMEM((ROUNDS, 2, 8, 2 * lines), F32),
+            pltpu.VMEM(field.shape, F32),
+            pltpu.VMEM(field.shape, F32),
+            pltpu.SemaphoreType.DMA((8,)),
+            pltpu.SemaphoreType.DMA((2,)),
             pltpu.SemaphoreType.DMA((n,)),
             pltpu.SemaphoreType.DMA((n,)),
             pltpu.SemaphoreType.DMA((ROUNDS, 4)),
             pltpu.SemaphoreType.DMA((ROUNDS, 4)),
         ],
         compiler_params=pltpu.CompilerParams(
-            collective_id=0, has_side_effects=True, vmem_limit_bytes=48 * 1024 * 1024
+            collective_id=0, has_side_effects=True, vmem_limit_bytes=64 * 1024 * 1024
         ),
-    )(
-        rhs_field.reshape(field.shape), permittivity, surf_dist, surf_normal, surf_inc,
-        surf_cell, surf_mask, surf_owner,
-    )
+    )(*operands)
+    sol, res = pl.pallas_call(
+        write_out,
+        out_shape=(field, field),
+        in_specs=[hbm] * 2,
+        out_specs=(hbm, hbm),
+        scratch_shapes=[pltpu.SemaphoreType.DMA((2,))],
+        compiler_params=pltpu.CompilerParams(vmem_limit_bytes=64 * 1024 * 1024),
+    )(sol, res)
     return sol.reshape(rhs_field.shape), res.reshape(rhs_field.shape)
 
 

time: 34.7 us -> 37.6 us (1.084)
  Pallas kernels: 26.8 us -> 36.8 us
  local copies, waits for them, and re-layouts: 6.77 us -> 0 us
    pallas_call x0 -> x1, Pallas kernels: none -> 9.06 us  [per_device(): pl.pallas_call(write_out, out_shape=(field, field), in_specs=[hbm] * 2, o...]
    unnamed x19 -> x0, local copies, waits for them, and re-layouts: 6.77 us -> none
    pallas_call x1, Pallas kernels: 26.8 us -> 27.7 us  [per_device(): pl.pallas_call(functools.partial(kernel, n_gx, n_gy), out_shape=(field, f...]
where the time goes in v2:
time: 37.6 us; the launch traced here: 37.4 us
  Pallas kernels  36.8 us (98%)
  between operations  0.64 us (2%)
    pallas_call x1, Pallas kernels, per_device(): pl.pallas_call(functools.partial(kernel, n_gx, n_gy), out_shape=(field, f...  27.7 us
    pallas_call x1, Pallas kernels, per_device(): pl.pallas_call(write_out, out_shape=(field, field), in_specs=[hbm] * 2, o...  9.06 us

profile of v2, /device:TPU:0, one launch (start us, length us, event | category | flops | bytes accessed | tf_op | source)
XLA Modules:
  0.0 37.4 jit_solution(13652845080894378282)
XLA Ops:
  0.6 27.7 %shard_map.95 = (f32[16,8,256]{2,1,0:T(8,128)}, f32[16,8,256]{2,1,0:T(8,128)}) custom-call(f32[16,8,256]{2,1,0:T(8,128)} %bitcast.4, f32[8,8,256]{2,1,0:T(8,128)} %perm_hbm.1, f32[32,128]{1,0:T(8,128)} %dist_hbm.1, f32[3,32,128]{2,1,0:T(8,128)} %normal_hbm.1, f32[2,32,128]{2,1,0:T(8,128)} %inc_hbm.1, s32[32,128]{1,0:T(8,128)} %cell_hbm.1, ...), custom_call_target="tpu_custom_call" | custom-call | tf_op jit(solution)/shard_map/pallas_call | solution.py:304
  28.4 9.1 %shard_map.96 = (f32[16,8,256]{2,1,0:T(8,128)}, f32[16,8,256]{2,1,0:T(8,128)}) custom-call(f32[16,8,256]{2,1,0:T(8,128)} %get-tuple-element.6.sol_ref, f32[16,8,256]{2,1,0:T(8,128)} %get-tuple-element.7.res_ref), custom_call_target="tpu_custom_call" | custom-call | tf_op jit(solution)/shard_map/pallas_call | solution.py:333

commit v3 on v2

--- a/solution.py
+++ b/solution.py
@@ -274,15 +274,22 @@
     sol_write.wait()
 
 
-def write_out(sol_ref, res_ref, sol_hbm, res_hbm, done):
-    copies = (
-        pltpu.make_async_copy(sol_ref, sol_hbm, done.at[0]),
-        pltpu.make_async_copy(res_ref, res_hbm, done.at[1]),
-    )
-    for copy in copies:
-        copy.start()
-    for copy in copies:
-        copy.wait()
+def write_out(sol_ref, res_ref, sol_out, res_out, sol_held, res_held, here, done):
+    loads = (
+        pltpu.make_async_copy(sol_ref, sol_held, here.at[0]),
+        pltpu.make_async_copy(res_ref, res_held, here.at[1]),
+    )
+    stores = (
+        pltpu.make_async_copy(sol_held, sol_out, done.at[0]),
+        pltpu.make_async_copy(res_held, res_out, done.at[1]),
+    )
+    for load in loads:
+        load.start()
+    for load, store in zip(loads, stores):
+        load.wait()
+        store.start()
+    for store in stores:
+        store.wait()
 
 
 def per_device(
@@ -335,7 +342,12 @@
         out_shape=(field, field),
         in_specs=[hbm] * 2,
         out_specs=(hbm, hbm),
-        scratch_shapes=[pltpu.SemaphoreType.DMA((2,))],
+        scratch_shapes=[
+            pltpu.VMEM(field.shape, F32),
+            pltpu.VMEM(field.shape, F32),
+            pltpu.SemaphoreType.DMA((2,)),
+            pltpu.SemaphoreType.DMA((2,)),
+        ],
         compiler_params=pltpu.CompilerParams(vmem_limit_bytes=64 * 1024 * 1024),
     )(sol, res)
     return sol.reshape(rhs_field.shape), res.reshape(rhs_field.shape)

time: 37.6 us -> 30.2 us (0.80)
  Pallas kernels: 36.8 us -> 29.4 us
    pallas_call x1, Pallas kernels: 9.06 us -> 1.66 us  [per_device(): pl.pallas_call(write_out, out_shape=(field, field), in_specs=[hbm] * 2, o...]
where the time goes in v3:
time: 30.2 us; the launch traced here: 30 us
  Pallas kernels  29.4 us (97%)
  between operations  0.64 us (2%)
    pallas_call x1, Pallas kernels, per_device(): pl.pallas_call(functools.partial(kernel, n_gx, n_gy), out_shape=(field, f...  27.7 us
    pallas_call x1, Pallas kernels, per_device(): pl.pallas_call(write_out, out_shape=(field, field), in_specs=[hbm] * 2, o...  1.66 us

profile of v3, /device:TPU:0, one launch (start us, length us, event | category | flops | bytes accessed | tf_op | source)
XLA Modules:
  0.0 30.0 jit_solution(7654360272848991915)
XLA Ops:
  0.6 27.7 %shard_map.95 = (f32[16,8,256]{2,1,0:T(8,128)}, f32[16,8,256]{2,1,0:T(8,128)}) custom-call(f32[16,8,256]{2,1,0:T(8,128)} %bitcast.4, f32[8,8,256]{2,1,0:T(8,128)} %perm_hbm.1, f32[32,128]{1,0:T(8,128)} %dist_hbm.1, f32[3,32,128]{2,1,0:T(8,128)} %normal_hbm.1, f32[2,32,128]{2,1,0:T(8,128)} %inc_hbm.1, s32[32,128]{1,0:T(8,128)} %cell_hbm.1, ...), custom_call_target="tpu_custom_call" | custom-call | tf_op jit(solution)/shard_map/pallas_call | solution.py:311
  28.4 1.7 %shard_map.96 = (f32[16,8,256]{2,1,0:T(8,128)}, f32[16,8,256]{2,1,0:T(8,128)}) custom-call(f32[16,8,256]{2,1,0:T(8,128)} %get-tuple-element.6.sol_ref, f32[16,8,256]{2,1,0:T(8,128)} %get-tuple-element.7.res_ref), custom_call_target="tpu_custom_call" | custom-call | tf_op jit(solution)/shard_map/pallas_call | solution.py:340

commit v4 on v3

--- a/solution.py
+++ b/solution.py
@@ -17,7 +17,7 @@
 ROWS = -(-SENT // 8) * 8
 PARTS = 11
 GROUP = 8
-ROUNDS = 3
+REACH = 3
 MESH = pl.DeviceIdType.MESH
 F32 = jnp.float32
 BF16 = jnp.bfloat16
@@ -32,7 +32,7 @@
     rhs_hbm, perm_hbm, dist_hbm, normal_hbm, inc_hbm, cell_hbm, mask_hbm, owner_hbm,
     sol_hbm, res_hbm,
     rhs_ref, perm_ref, dist_ref, normal_ref, inc_ref, cell_ref, mask_ref, owner_ref,
-    send, recv, left, right, acc, row_send, row_recv, col_send, col_recv,
+    send, recv, left, right, acc, right_ref, right_row, slope_ref, slope_row, perm_row, strip_send, strip_recv,
     sol_ref, res_ref, loaded, written, block_out, block_in, halo_out, halo_in,
 ):
     gx, gy = lax.axis_index("gx"), lax.axis_index("gy")
@@ -118,29 +118,80 @@
     for load in loads[6:]:
         load.wait()
 
-    @pl.when(gx == 0)
-    def _():
-        row_recv[:, 0] = jnp.zeros((ROUNDS, 2 * planes, cols), F32)
-
-    @pl.when(gx == n_gx - 1)
-    def _():
-        row_recv[:, 1] = jnp.zeros((ROUNDS, 2 * planes, cols), F32)
-
-    @pl.when(gy == 0)
-    def _():
-        col_recv[:, 0] = jnp.zeros((ROUNDS, 8, 2 * lines), F32)
-
-    @pl.when(gy == n_gy - 1)
-    def _():
-        col_recv[:, 1] = jnp.zeros((ROUNDS, 8, 2 * lines), F32)
-
-    perm = perm_ref[...]
-    diag = 6.0 - K_SQUARED * perm
-    shift = BETA * K_SQUARED * perm
-    denom = diag * diag + shift * shift
-    inv_real = diag / denom
-    inv_imag = -shift / denom
-    both_diag = jnp.concatenate([diag, diag], axis=0)
+    def within(x, y):
+        return (x >= 0) & (x < n_gx) & (y >= 0) & (y < n_gy)
+
+    def strips(first, field):
+        flat = field.reshape(2 * lines, cols)
+        strip_send[0, first] = jnp.transpose(flat[:, cols - 128:])[120:128]
+        strip_send[1, first] = jnp.transpose(flat[:, :128])[0:8]
+
+    def edge_copies(early):
+        moves = []
+        for side, dx in enumerate((1, -1)):
+            top = rows - REACH if dx == 1 else 0
+            end = rows - 1 if dx == 1 else 0
+            if early:
+                moves.append((dx, 0, perm_ref.at[:, pl.ds(top, REACH)], perm_row.at[:, pl.ds(top, REACH)]))
+            else:
+                moves.append((dx, 0, right_ref.at[:, pl.ds(top, REACH)], right_row.at[:, pl.ds(top, REACH)]))
+                moves.append((dx, 0, slope_ref.at[:, pl.ds(end, 1)], slope_row.at[:, pl.ds(end, 1)]))
+        part = pl.ds(0, 1) if early else pl.ds(1, 3)
+        for side, dy in enumerate((1, -1)):
+            for dx in (-1, 0, 1):
+                moves.append((dx, dy, strip_send.at[side, part], strip_recv.at[side, dx + 1, part]))
+        out = []
+        for number, (dx, dy, source, sink) in enumerate(moves):
+            which = (0 if early else 1, number)
+            out.append((
+                within(gx + dx, gy + dy), within(gx - dx, gy - dy),
+                pltpu.make_async_remote_copy(
+                    src_ref=source, dst_ref=sink,
+                    send_sem=halo_out.at[which], recv_sem=halo_in.at[which],
+                    device_id=(gx + dx, gy + dy), device_id_type=MESH,
+                ),
+            ))
+        return out
+
+    def start_edges(copies):
+        for there, _, copy in copies:
+            pl.when(there)(copy.start)
+
+    def finish_edges(copies):
+        for there, comes, copy in copies:
+            pl.when(comes)(copy.wait_recv)
+
+    def beside_tile(dx, first):
+        empty = jnp.zeros((112, 2 * lines), F32)
+        stacked = jnp.concatenate(
+            [strip_recv[1, dx + 1, first], empty, strip_recv[0, dx + 1, first]], axis=0
+        )
+        return jnp.transpose(stacked).reshape(2 * planes, rows, 128)
+
+    size = (2 * planes, rows, cols + 128)
+    row_at, col_at = iota(size, 1), iota(size, 2)
+    other = iota(size, 0) >= planes
+    row_own = jnp.where(other, jnp.where(row_at < 4, rows + row_at, row_at - rows), row_at)
+    col_own = jnp.where(col_at < cols + 64, col_at, col_at - (cols + 128))
+    row_all, col_all = gx * rows + row_own, gy * cols + col_own
+    inside = (row_all >= 0) & (row_all < n_gx * rows) & (col_all >= 0) & (col_all < n_gy * cols)
+    valid = inside & (row_own >= -REACH) & (row_own < rows + REACH)
+
+    def extended(own, around, first, part, corners=True):
+        at = slice(part * planes, (part + 1) * planes)
+        side = beside_tile(0, first)[at]
+        if corners:
+            near = iota((planes, rows, 128), 1) < 4
+            far = jnp.where(near, beside_tile(-1, first)[at], beside_tile(1, first)[at])
+        else:
+            far = jnp.zeros(side.shape, F32)
+        return jnp.concatenate([
+            jnp.concatenate([own, side], axis=2), jnp.concatenate([around, far], axis=2)
+        ], axis=0)
+
+    strips(0, jnp.concatenate([perm_ref[...], perm_ref[...]], axis=0))
+    early_copies = edge_copies(True)
+    start_edges(early_copies)
 
     acc[...] = jnp.zeros(acc.shape, F32)
     line_no = iota((lines, points), 0).astype(F32)
@@ -183,87 +234,86 @@
         both = acc[top:top + lines, :] + acc[top + lines:top + 2 * lines, :]
         return both.reshape(planes, rows, cols)
 
-    def twice(x):
-        return jnp.concatenate([x, x], axis=0)
-
-    def precond(vec):
-        real, imag = vec[:planes], vec[planes:]
-        return jnp.concatenate(
-            [real * inv_real - imag * inv_imag, real * inv_imag + imag * inv_real], axis=0
+    finish_edges(early_copies)
+    perm = jnp.where(valid, extended(perm_ref[...], perm_row[...], 0, 0), 0.0)
+    diag = 6.0 - K_SQUARED * perm
+    shift = BETA * K_SQUARED * perm
+    denom = diag * diag + shift * shift
+    inv_real = diag / denom
+    inv_imag = -shift / denom
+
+    right_ref[0:planes] = rhs_ref[0:planes] - summed(3)
+    right_ref[planes:] = rhs_ref[planes:] - summed(4)
+    slope_ref[0:planes] = acc[0:lines, :].reshape(planes, rows, cols)
+    for f in range(3):
+        slope_ref[(1 + f) * planes:(2 + f) * planes] = summed(f)
+    strips(1, right_ref[...])
+    strips(2, slope_ref[0:2 * planes])
+    strips(3, slope_ref[2 * planes:])
+    late_copies = edge_copies(False)
+    start_edges(late_copies)
+    finish_edges(late_copies)
+
+    def right_part(part):
+        at = slice(part * planes, (part + 1) * planes)
+        return jnp.where(valid, extended(right_ref[at], right_row[at], 1, part), 0.0)
+
+    def slope(f):
+        at = slice(f * planes, (f + 1) * planes)
+        return extended(slope_ref[at], slope_row[at], 2 + f // 2, f % 2, corners=False)
+
+    def precond(real, imag):
+        return (
+            OMEGA * (real * inv_real - imag * inv_imag),
+            OMEGA * (real * inv_imag + imag * inv_real),
         )
 
-    def halo_copies(step):
-        out = []
-        for side, (there, dx, dy) in enumerate(
-            ((gx < n_gx - 1, 1, 0), (gx > 0, -1, 0), (gy < n_gy - 1, 0, 1), (gy > 0, 0, -1))
-        ):
-            source, sink = (row_send, row_recv) if side < 2 else (col_send, col_recv)
-            out.append((there, pltpu.make_async_remote_copy(
-                src_ref=source.at[step, side % 2], dst_ref=sink.at[step, side % 2],
-                send_sem=halo_out.at[step, side], recv_sem=halo_in.at[step, side],
-                device_id=(gx + dx, gy + dy), device_id_type=MESH,
-            )))
-        return out
-
-    full = (2 * planes, rows, cols)
-    row_at, col_at = iota(full, 1), iota(full, 2)
-
-    def beside(step, v):
-        flat = v.reshape(2 * lines, cols)
-        row_send[step, 0] = v[:, rows - 1, :]
-        row_send[step, 1] = v[:, 0, :]
-        col_send[step, 0] = jnp.transpose(flat[:, cols - 128:])[120:128]
-        col_send[step, 1] = jnp.transpose(flat[:, :128])[0:8]
-        copies = halo_copies(step)
-        for there, copy in copies:
-            pl.when(there)(copy.start)
-        zero = jnp.zeros((1, rows, cols), F32)
+    def swapped(v):
+        return jnp.concatenate([v[planes:], v[:planes]], axis=0)
+
+    def shifts(v):
+        zero = jnp.zeros((1, *size[1:]), F32)
         z_next = jnp.concatenate([v[1:planes], zero, v[planes + 1:], zero], axis=0)
         z_last = jnp.concatenate([zero, v[:planes - 1], zero, v[planes:-1]], axis=0)
         x_next = pltpu.roll(v, rows - 1, 1)
+        x_next = jnp.where(row_at == rows - 1, swapped(x_next), x_next)
         x_last = pltpu.roll(v, 1, 1)
-        y_next = pltpu.roll(v, cols - 1, 2)
-        y_last = pltpu.roll(v, 1, 2)
-        for side, (there, copy) in enumerate(copies):
-            comes = copies[side ^ 1][0]
-            pl.when(comes)(copy.wait_recv)
-            pl.when(there)(copy.wait_send)
-        x_last = jnp.where(row_at == 0, row_recv[step, 0][:, None, :], x_last)
-        x_next = jnp.where(row_at == rows - 1, row_recv[step, 1][:, None, :], x_next)
-
-        def edge(row):
-            column = jnp.transpose(jnp.broadcast_to(row, (2 * lines, 2 * lines)))
-            return jnp.concatenate([column] * (cols // (2 * lines)), axis=1).reshape(full)
-
-        y_last = jnp.where(col_at == 0, edge(col_recv[step, 0, 7:8, :]), y_last)
-        y_next = jnp.where(col_at == cols - 1, edge(col_recv[step, 1, 0:1, :]), y_next)
-        return z_next, z_last, x_next, x_last, y_next, y_last
+        x_last = jnp.where(row_at == 0, swapped(x_last), x_last)
+        return z_next, z_last, x_next, x_last, pltpu.roll(v, size[2] - 1, 2), pltpu.roll(v, 1, 2)
 
     def helm(v, around):
         z_next, z_last, x_next, x_last, y_next, y_last = around
-        return both_diag * v - (z_next + z_last + x_next + x_last + y_next + y_last)
-
-    def sweep(step, z, residual):
-        image = helm(z, beside(step, z))
-        real = image[:planes] - shift * z[planes:]
-        imag = image[planes:] + shift * z[:planes]
-        return z + OMEGA * precond(residual - jnp.concatenate([real, imag], axis=0))
-
-    source = rhs_ref[...] - jnp.concatenate([summed(3), summed(4)], axis=0)
-    solution = sweep(0, OMEGA * precond(source), source)
-    around = beside(1, solution)
-    z_next, z_last, x_next, x_last, y_next, y_last = around
-    surface = twice(acc[0:lines, :].reshape(planes, rows, cols)) * solution
-    surface = surface + twice(summed(0)) * (z_next - z_last)
-    surface = surface + twice(summed(1)) * (x_next - x_last)
-    surface = surface + twice(summed(2)) * (y_next - y_last)
-    residual = source - helm(solution, around) - surface
-    res_ref[...] = residual
+        return diag * v - (z_next + z_last + x_next + x_last + y_next + y_last)
+
+    def update(real, imag):
+        z_real, z_imag = precond(real, imag)
+        image_real = helm(z_real, shifts(z_real)) - shift * z_imag
+        image_imag = helm(z_imag, shifts(z_imag)) + shift * z_real
+        more_real, more_imag = precond(real - image_real, imag - image_imag)
+        return z_real + more_real, z_imag + more_imag
+
+    source = right_part(0), right_part(1)
+    first = [jnp.where(inside, v, 0.0) for v in update(*source)]
+    slopes = [slope(f) for f in range(4)]
+    residual = []
+    for v, origin in zip(first, source):
+        around = shifts(v)
+        z_next, z_last, x_next, x_last, y_next, y_last = around
+        surface = slopes[0] * v + slopes[1] * (z_next - z_last)
+        surface = surface + slopes[2] * (x_next - x_last) + slopes[3] * (y_next - y_last)
+        residual.append(jnp.where(inside, origin - helm(v, around) - surface, 0.0))
+    for part in range(2):
+        res_ref[part * planes:(part + 1) * planes] = residual[part][:planes, :, :cols]
     res_write = pltpu.make_async_copy(res_ref, res_hbm, written.at[0])
     res_write.start()
-    sol_ref[...] = solution + sweep(2, OMEGA * precond(residual), residual)
+    second = update(*residual)
+    for part in range(2):
+        both = first[part] + second[part]
+        sol_ref[part * planes:(part + 1) * planes] = both[:planes, :, :cols]
     sol_write = pltpu.make_async_copy(sol_ref, sol_hbm, written.at[1])
     sol_write.start()
+    for there, _, copy in early_copies + late_copies:
+        pl.when(there)(copy.wait_send)
 
     def finish_block(k, carry):
         block_copy(k).wait_send()
@@ -320,18 +370,21 @@
             pltpu.VMEM((PARTS * lines, deep), BF16),
             pltpu.VMEM((cols, deep), BF16),
             pltpu.VMEM((PARTS * lines, cols), F32),
-            pltpu.VMEM((ROUNDS, 2, 2 * planes, cols), F32),
-            pltpu.VMEM((ROUNDS, 2, 2 * planes, cols), F32),
-            pltpu.VMEM((ROUNDS, 2, 8, 2 * lines), F32),
-            pltpu.VMEM((ROUNDS, 2, 8, 2 * lines), F32),
+            pltpu.VMEM((2 * planes, rows, cols), F32),
+            pltpu.VMEM((2 * planes, rows, cols), F32),
+            pltpu.VMEM((4 * planes, rows, cols), F32),
+            pltpu.VMEM((4 * planes, rows, cols), F32),
+            pltpu.VMEM((planes, rows, cols), F32),
+            pltpu.VMEM((2, 4, 8, 2 * lines), F32),
+            pltpu.VMEM((2, 3, 4, 8, 2 * lines), F32),
             pltpu.VMEM(field.shape, F32),
             pltpu.VMEM(field.shape, F32),
             pltpu.SemaphoreType.DMA((8,)),
             pltpu.SemaphoreType.DMA((2,)),
             pltpu.SemaphoreType.DMA((n,)),
             pltpu.SemaphoreType.DMA((n,)),
-            pltpu.SemaphoreType.DMA((ROUNDS, 4)),
-            pltpu.SemaphoreType.DMA((ROUNDS, 4)),
+            pltpu.SemaphoreType.DMA((2, 10)),
+            pltpu.SemaphoreType.DMA((2, 10)),
         ],
         compiler_params=pltpu.CompilerParams(
             collective_id=0, has_side_effects=True, vmem_limit_bytes=64 * 1024 * 1024

time: 30.2 us -> 26.9 us (0.89)
  the two profiles are of different devices: /device:TPU:0 before, /device:TPU:3 now
where the time goes in v4:
time: 26.9 us; the launch traced here: 26.7 us
  Pallas kernels  26.1 us (97%)
  between operations  0.64 us (2%)
    pallas_call x1, Pallas kernels, per_device(): pl.pallas_call(functools.partial(kernel, n_gx, n_gy), out_shape=(field, f...  24.4 us
    pallas_call x1, Pallas kernels, per_device(): pl.pallas_call(write_out, out_shape=(field, field), in_specs=[hbm] * 2, o...  1.66 us

profile of v4, /device:TPU:3, one launch (start us, length us, event | category | flops | bytes accessed | tf_op | source)
XLA Modules:
  0.0 26.7 jit_solution(13754054545576924701)
XLA Ops:
  0.6 24.4 %shard_map.95 = (f32[16,8,256]{2,1,0:T(8,128)}, f32[16,8,256]{2,1,0:T(8,128)}) custom-call(f32[16,8,256]{2,1,0:T(8,128)} %bitcast.4, f32[8,8,256]{2,1,0:T(8,128)} %perm_hbm.1, f32[32,128]{1,0:T(8,128)} %dist_hbm.1, f32[3,32,128]{2,1,0:T(8,128)} %normal_hbm.1, f32[2,32,128]{2,1,0:T(8,128)} %inc_hbm.1, s32[32,128]{1,0:T(8,128)} %cell_hbm.1, ...), custom_call_target="tpu_custom_call" | custom-call | tf_op jit(solution)/shard_map/pallas_call | solution.py:361
  25.0 1.7 %shard_map.96 = (f32[16,8,256]{2,1,0:T(8,128)}, f32[16,8,256]{2,1,0:T(8,128)}) custom-call(f32[16,8,256]{2,1,0:T(8,128)} %get-tuple-element.6.sol_ref, f32[16,8,256]{2,1,0:T(8,128)} %get-tuple-element.7.res_ref), custom_call_target="tpu_custom_call" | custom-call | tf_op jit(solution)/shard_map/pallas_call | solution.py:393

commit v5 on v4

--- a/solution.py
+++ b/solution.py
@@ -194,8 +194,13 @@
     start_edges(early_copies)
 
     acc[...] = jnp.zeros(acc.shape, F32)
-    line_no = iota((lines, points), 0).astype(F32)
-    col_no = iota((cols, points), 0).astype(F32)
+    line_no = iota((lines, points), 0).astype(F32).astype(BF16)
+    col_no = iota((cols, points), 0).astype(F32).astype(BF16)
+    one, nil = jnp.ones((), BF16), jnp.zeros((), BF16)
+
+    def spread(row, count):
+        some = jnp.broadcast_to(row, (16, points)).astype(BF16)
+        return jnp.concatenate([some] * (count // 16), axis=0)
 
     def gather_group(g, carry):
         for j in range(GROUP):
@@ -212,16 +217,15 @@
                 cell = tile[0:1]
                 line = jnp.floor(cell * (1.0 / cols))
                 column = cell - line * cols
-                right[:, at] = jnp.where(col_no == column, 1.0, 0.0).astype(BF16)
-                here = line_no == line
-                left[0:lines, at] = jnp.where(here, tile[1:2], 0.0).astype(BF16)
+                right[:, at] = jnp.where(col_no == spread(column, cols), one, nil)
+                here = jnp.where(line_no == spread(line, lines), one, nil)
+                left[0:lines, at] = here * spread(tile[1:2], lines)
                 upper = tile.astype(BF16).astype(F32)
                 lower = tile - upper
                 for f in range(5):
                     for p, part in enumerate((upper, lower)):
                         top = (1 + 2 * f + p) * lines
-                        value = jnp.where(here, part[2 + f:3 + f], 0.0)
-                        left[top:top + lines, at] = value.astype(BF16)
+                        left[top:top + lines, at] = here * spread(part[2 + f:3 + f], lines)
         acc[...] += lax.dot_general(
             left[...], right[...], (((1,), (1,)), ((), ())), preferred_element_type=F32
         )

time: 26.9 us -> 25.9 us (0.963)
  Pallas kernels: 26.1 us -> 25.2 us
    pallas_call x1, Pallas kernels: 24.4 us -> 23.5 us  [per_device(): pl.pallas_call(functools.partial(kernel, n_gx, n_gy), out_shape=(field, f...]
where the time goes in v5:
time: 25.9 us; the launch traced here: 25.8 us
  Pallas kernels  25.2 us (97%)
  between operations  0.64 us (2%)
    pallas_call x1, Pallas kernels, per_device(): pl.pallas_call(functools.partial(kernel, n_gx, n_gy), out_shape=(field, f...  23.5 us
    pallas_call x1, Pallas kernels, per_device(): pl.pallas_call(write_out, out_shape=(field, field), in_specs=[hbm] * 2, o...  1.66 us

profile of v5, /device:TPU:3, one launch (start us, length us, event | category | flops | bytes accessed | tf_op | source)
XLA Modules:
  0.0 25.8 jit_solution(13159322985424733713)
XLA Ops:
  0.6 23.5 %shard_map.95 = (f32[16,8,256]{2,1,0:T(8,128)}, f32[16,8,256]{2,1,0:T(8,128)}) custom-call(f32[16,8,256]{2,1,0:T(8,128)} %bitcast.4, f32[8,8,256]{2,1,0:T(8,128)} %perm_hbm.1, f32[32,128]{1,0:T(8,128)} %dist_hbm.1, f32[3,32,128]{2,1,0:T(8,128)} %normal_hbm.1, f32[2,32,128]{2,1,0:T(8,128)} %inc_hbm.1, s32[32,128]{1,0:T(8,128)} %cell_hbm.1, ...), custom_call_target="tpu_custom_call" | custom-call | tf_op jit(solution)/shard_map/pallas_call | solution.py:365
  24.1 1.7 %shard_map.96 = (f32[16,8,256]{2,1,0:T(8,128)}, f32[16,8,256]{2,1,0:T(8,128)}) custom-call(f32[16,8,256]{2,1,0:T(8,128)} %get-tuple-element.6.sol_ref, f32[16,8,256]{2,1,0:T(8,128)} %get-tuple-element.7.res_ref), custom_call_target="tpu_custom_call" | custom-call | tf_op jit(solution)/shard_map/pallas_call | solution.py:397

commit v6 on v5

--- a/solution.py
+++ b/solution.py
@@ -231,13 +231,8 @@
         )
         return carry
 
-    lax.fori_loop(0, n // GROUP, gather_group, 0)
-
-    def summed(f):
-        top = (1 + 2 * f) * lines
-        both = acc[top:top + lines, :] + acc[top + lines:top + 2 * lines, :]
-        return both.reshape(planes, rows, cols)
-
+    groups = n // GROUP
+    lax.fori_loop(0, groups - 1, gather_group, 0)
     finish_edges(early_copies)
     perm = jnp.where(valid, extended(perm_ref[...], perm_row[...], 0, 0), 0.0)
     diag = 6.0 - K_SQUARED * perm
@@ -245,6 +240,12 @@
     denom = diag * diag + shift * shift
     inv_real = diag / denom
     inv_imag = -shift / denom
+    gather_group(groups - 1, 0)
+
+    def summed(f):
+        top = (1 + 2 * f) * lines
+        both = acc[top:top + lines, :] + acc[top + lines:top + 2 * lines, :]
+        return both.reshape(planes, rows, cols)
 
     right_ref[0:planes] = rhs_ref[0:planes] - summed(3)
     right_ref[planes:] = rhs_ref[planes:] - summed(4)

time: 25.9 us -> 26 us (level)
  no operation moved by 1% of the time
where the time goes in v6:
time: 26 us; the launch traced here: 25.8 us
  Pallas kernels  25.2 us (97%)
  between operations  0.64 us (2%)
    pallas_call x1, Pallas kernels, per_device(): pl.pallas_call(functools.partial(kernel, n_gx, n_gy), out_shape=(field, f...  23.5 us
    pallas_call x1, Pallas kernels, per_device(): pl.pallas_call(write_out, out_shape=(field, field), in_specs=[hbm] * 2, o...  1.66 us

profile of v6, /device:TPU:3, one launch (start us, length us, event | category | flops | bytes accessed | tf_op | source)
XLA Modules:
  0.0 25.8 jit_solution(12299356598835064520)
XLA Ops:
  0.6 23.5 %shard_map.95 = (f32[16,8,256]{2,1,0:T(8,128)}, f32[16,8,256]{2,1,0:T(8,128)}) custom-call(f32[16,8,256]{2,1,0:T(8,128)} %bitcast.4, f32[8,8,256]{2,1,0:T(8,128)} %perm_hbm.1, f32[32,128]{1,0:T(8,128)} %dist_hbm.1, f32[3,32,128]{2,1,0:T(8,128)} %normal_hbm.1, f32[2,32,128]{2,1,0:T(8,128)} %inc_hbm.1, s32[32,128]{1,0:T(8,128)} %cell_hbm.1, ...), custom_call_target="tpu_custom_call" | custom-call | tf_op jit(solution)/shard_map/pallas_call | solution.py:366
  24.2 1.7 %shard_map.96 = (f32[16,8,256]{2,1,0:T(8,128)}, f32[16,8,256]{2,1,0:T(8,128)}) custom-call(f32[16,8,256]{2,1,0:T(8,128)} %get-tuple-element.6.sol_ref, f32[16,8,256]{2,1,0:T(8,128)} %get-tuple-element.7.res_ref), custom_call_target="tpu_custom_call" | custom-call | tf_op jit(solution)/shard_map/pallas_call | solution.py:398

commit v7 on v5

--- a/solution.py
+++ b/solution.py
@@ -16,7 +16,7 @@
 SENT = CAP * FIELDS
 ROWS = -(-SENT // 8) * 8
 PARTS = 11
-GROUP = 8
+GROUP = 4
 REACH = 3
 MESH = pl.DeviceIdType.MESH
 F32 = jnp.float32

time: 25.9 us -> 26 us (level)
  no operation moved by 1% of the time
where the time goes in v7:
time: 26 us; the launch traced here: 25.8 us
  Pallas kernels  25.2 us (97%)
  between operations  0.64 us (2%)
    pallas_call x1, Pallas kernels, per_device(): pl.pallas_call(functools.partial(kernel, n_gx, n_gy), out_shape=(field, f...  23.5 us
    pallas_call x1, Pallas kernels, per_device(): pl.pallas_call(write_out, out_shape=(field, field), in_specs=[hbm] * 2, o...  1.66 us

profile of v7, /device:TPU:3, one launch (start us, length us, event | category | flops | bytes accessed | tf_op | source)
XLA Modules:
  0.0 25.8 jit_solution(570905409422707478)
XLA Ops:
  0.6 23.5 %shard_map.95 = (f32[16,8,256]{2,1,0:T(8,128)}, f32[16,8,256]{2,1,0:T(8,128)}) custom-call(f32[16,8,256]{2,1,0:T(8,128)} %bitcast.4, f32[8,8,256]{2,1,0:T(8,128)} %perm_hbm.1, f32[32,128]{1,0:T(8,128)} %dist_hbm.1, f32[3,32,128]{2,1,0:T(8,128)} %normal_hbm.1, f32[2,32,128]{2,1,0:T(8,128)} %inc_hbm.1, s32[32,128]{1,0:T(8,128)} %cell_hbm.1, ...), custom_call_target="tpu_custom_call" | custom-call | tf_op jit(solution)/shard_map/pallas_call | solution.py:365
  24.2 1.7 %shard_map.96 = (f32[16,8,256]{2,1,0:T(8,128)}, f32[16,8,256]{2,1,0:T(8,128)}) custom-call(f32[16,8,256]{2,1,0:T(8,128)} %get-tuple-element.6.sol_ref, f32[16,8,256]{2,1,0:T(8,128)} %get-tuple-element.7.res_ref), custom_call_target="tpu_custom_call" | custom-call | tf_op jit(solution)/shard_map/pallas_call | solution.py:397
